TPU v7x, 256 devices: a whole 4x4x8 slice. The times are simulated.
256 devices in a mesh: sect: 4 (over z_hi), ctx: 8 (over z_lo, y), tp: 8 (over x, core).
Axes of the slice: x: 4, y: 4, z: 8 (z_hi: 4, z_lo: 2; z = z_hi * 2 + z_lo), core: 2. Of those that a mesh axis runs over, the one named last changes fastest.
Arguments:
- patches: bfloat16 [4096, 1280], P(('sect', 'ctx')), may hold values from -6 to 6
- patch_gain: float32 [1280], replicated, may hold values from 0.25 to 1.75
- patch_shift: float32 [1280], replicated, may hold values from -3 to 3
- encoder_up: bfloat16 [1280, 5120], P(None, 'tp'), may hold values from -0.15625 to 0.15625
- encoder_down: bfloat16 [5120, 1280], P('tp'), may hold values from -0.078125 to 0.078125
- proj_weight: bfloat16 [1280, 8192], P(None, 'tp'), may hold values from -0.15625 to 0.15625
- hidden_text: bfloat16 [8192, 8192], P(('sect', 'ctx'), 'tp'), may hold values from -180 to 180
- slot_source: int32 [64], P(('sect', 'ctx')), may hold values from 0 to 4, as said below
- norm_gain: float32 [8192], P('tp'), may hold values from 0.25 to 1.75
- kv_weight: bfloat16 [2048, 8192], P(None, 'tp'), may hold values from -0.0625 to 0.0625
- queries: bfloat16 [8192, 4096], P(('sect', 'ctx'), 'tp'), may hold values from -40 to 40
Outputs:
- attended: bfloat16 [8192, 4096], P(('sect', 'ctx'), 'tp')
Inputs may be any that keep to these rules, and one draw needn't show every extreme that they name: `slot_source`: for each ctx index, the slots of the blocks with that index carry each value 0 to 3 exactly once, all other slots 4.
All inputs are finite; a program needn't handle non-finite values.
Results may differ from a plain program's by a relative error of at most 0.019.
Values may be sent and summed in bfloat16 or wider, within the bound.
No kernel may reach another device: no remote copies, remote signals or barrier semaphores. Data moves between devices by JAX's collectives and lax.ppermute only.
A program may use at most 128 MiB of HBM per device.

v0:
```python
from functools import partial
import math
import jax
import jax.numpy as jnp
from jax import lax
from jax.sharding import PartitionSpec as P

D = 8192
HEAD = 128
Q_HEADS = 32
KV_HEADS = 8
PATCHES = 128


def layer_norm(values, norm_scale, norm_shift):
    widened = values.astype(jnp.float32)
    center = jnp.mean(widened, axis=-1, keepdims=True)
    spread = jnp.mean(jnp.square(widened - center), axis=-1, keepdims=True)
    return ((widened - center) * lax.rsqrt(spread + 1e-06) * norm_scale + norm_shift).astype(
        jnp.bfloat16
    )


def rotate_keys(keys_in, positions):
    half_size = keys_in.shape[-2] // 2
    frequencies = jnp.exp(
        jnp.arange(half_size, dtype=jnp.float32) * (-2.0 * math.log(500000.0) / (2 * half_size))
    )
    angles = positions[None, :] * frequencies[:, None]
    cosine_table = jnp.cos(angles)
    sine_table = jnp.sin(angles)
    first_half = keys_in[..., :half_size, :]
    second_half = keys_in[..., half_size:, :]
    return jnp.concatenate(
        [
            first_half * cosine_table - second_half * sine_table,
            second_half * cosine_table + first_half * sine_table,
        ],
        axis=-2,
    )


def attend_update(state_now, queries_blk, query_pos, keys_blk, values_blk, key_pos):
    running_max, running_sum, accumulated = state_now
    scale_value = queries_blk.shape[-1] ** (-0.5)
    scores = (
        jnp.einsum("rkgd,kdn->kgrn", queries_blk, keys_blk, preferred_element_type=jnp.float32)
        * scale_value
    )
    allowed = query_pos[:, None] >= key_pos[None, :]
    scores = jnp.where(allowed, scores, -jnp.inf)
    new_max = jnp.maximum(running_max, jnp.max(scores, axis=-1))
    weights = jnp.exp(scores - new_max[..., None])
    running_sum = jnp.sum(weights, axis=-1)
    mixed_rows = jnp.einsum(
        "kgrn,kdn->kgrd",
        weights.astype(jnp.bfloat16),
        values_blk,
        preferred_element_type=jnp.float32,
    )
    accumulated = mixed_rows
    return (new_max, running_sum, accumulated)


def keep_state(state_now):
    return state_now


def fold_step(states, fragment, first_index, groups):
    key_tile, value_tile = fragment
    key_pos = jnp.arange(key_tile.shape[2], dtype=jnp.int32)
    updated = []
    for group_entry, state_now in zip(groups, states):
        group_queries, group_first = group_entry
        row_count = group_queries.shape[0]
        query_pos = group_first + jnp.arange(row_count, dtype=jnp.int32)
        runner = partial(
            attend_update,
            queries_blk=group_queries,
            query_pos=query_pos,
            keys_blk=key_tile,
            values_blk=value_tile,
            key_pos=key_pos,
        )
        updated.append(
            lax.cond(first_index <= group_first + row_count - 1, runner, keep_state, state_now)
        )
    return tuple(updated)


def initial_state(kv_count, group_size, row_count):
    return (
        jnp.full((kv_count, group_size, row_count), -1e30, jnp.float32),
        jnp.zeros((kv_count, group_size, row_count), jnp.float32),
        jnp.zeros((kv_count, group_size, row_count, HEAD), jnp.float32),
    )


def finish_state(state_now):
    final_max, final_sum, final_acc = state_now
    result = final_acc / final_sum[..., None]
    return jnp.transpose(result, (2, 0, 1, 3)).reshape(result.shape[2], -1).astype(jnp.bfloat16)


def body(
    patches,
    patch_gain,
    patch_shift,
    encoder_up,
    encoder_down,
    proj_weight,
    hidden_text,
    slot_source,
    norm_gain,
    kv_weight,
    queries,
):
    normed_patches = layer_norm(patches, patch_gain, patch_shift)
    enc_hidden = jax.nn.gelu(
        jnp.dot(normed_patches, encoder_up, preferred_element_type=jnp.float32), approximate=False
    ).astype(jnp.bfloat16)
    partial_out = jnp.dot(enc_hidden, encoder_down, preferred_element_type=jnp.float32)
    summed_out = lax.psum(partial_out, "tp")
    encoded = (patches.astype(jnp.float32) + summed_out).astype(jnp.bfloat16)
    image_emb = jnp.dot(encoded, proj_weight, preferred_element_type=jnp.float32).astype(
        jnp.bfloat16
    )
    slot_total = slot_source.shape[0]
    slots_start = hidden_text.reshape(slot_total, PATCHES, hidden_text.shape[1])
    current = slots_start
    fragment = lax.all_gather(image_emb, "sect", axis=0, tiled=True)
    first_source = jnp.int32(0) // PATCHES
    for offset in range(fragment.shape[0] // PATCHES):
        chosen = (slot_source == first_source + offset)[:, None, None]
        current = jnp.where(
            chosen, fragment[offset * PATCHES : (offset + 1) * PATCHES][None], current
        )
    merged = current.reshape(hidden_text.shape)
    widened = merged.astype(jnp.float32)
    square_sums = lax.psum(jnp.sum(jnp.square(widened), axis=1), "tp")
    inverse = lax.rsqrt(square_sums / D + 1e-05)
    normed_hidden = (widened * inverse[:, None] * norm_gain[None, :]).astype(jnp.bfloat16)
    head_rows = kv_weight.shape[0] // lax.axis_size("tp")
    projected = lax.psum_scatter(
        lax.dot_general(
            kv_weight, normed_hidden, (((1,), (1,)), ((), ())), preferred_element_type=jnp.float32
        ),
        "tp",
        scatter_dimension=0,
        tiled=True,
    )
    row_total = queries.shape[0]
    kv_count = head_rows // (2 * HEAD)
    projected = projected.reshape(kv_count, 2, HEAD, row_total)
    block_number = lax.axis_index(("sect", "ctx"))
    first_position = block_number * row_total
    positions = (first_position + jnp.arange(row_total, dtype=jnp.int32)).astype(jnp.float32)
    rotated = rotate_keys(projected[:, 0], positions).astype(jnp.bfloat16)
    value_rows = projected[:, 1].astype(jnp.bfloat16)
    group_size = Q_HEADS // KV_HEADS
    grouped_queries = queries.reshape(row_total, kv_count, group_size, HEAD)
    groups = ((grouped_queries, first_position),)
    initial = tuple(
        [initial_state(kv_count, group_size, group_entry[0].shape[0]) for group_entry in groups]
    )
    folder = partial(fold_step, groups=groups)
    finals = folder(
        initial,
        (
            lax.all_gather(rotated, ("sect", "ctx"), axis=2, tiled=True),
            lax.all_gather(value_rows, ("sect", "ctx"), axis=2, tiled=True),
        ),
        jnp.int32(0),
    )
    results = [finish_state(state_now) for state_now in finals]
    return results[0]


def solution(mesh):
    in_specs = (
        P(("sect", "ctx"), None),
        P(),
        P(),
        P(None, "tp"),
        P("tp", None),
        P(None, "tp"),
        P(("sect", "ctx"), "tp"),
        P(("sect", "ctx")),
        P("tp"),
        P(None, "tp"),
        P(("sect", "ctx"), "tp"),
    )
    out_specs = P(("sect", "ctx"), "tp")
    return jax.shard_map(body, mesh=mesh, in_specs=in_specs, out_specs=out_specs, check_vma=False)
```

profile of v0, /device:TPU:8, one launch (start us, length us, event | category | flops | bytes accessed | tf_op | source)
XLA Modules:
  0.0 383.6 jit_solution(16793101043001423742)
XLA Ops:
  6.5 0.0 copy-start
  6.5 0.0 all-reduce.2.cloned.1.call-start
  6.5 1.2 convert_reduce_fusion
  7.8 1.2 fusion.24
  9.0 0.0 copy-start.2
  9.0 4.4 %fusion.55 = f32[128,1280]{1,0:T(8,128)} fusion(bf16[640,1280]{1,0:T(8,128)(2,1)} %param.17, bf16[1280,640]{1,0:T(8,128)(2,1)} %param.16, bf16[128,1280]{1,0:T(8,128)(2,1)} %param.13, f32[1280]{0:T(1024)} %param.15, f32[1280]{0:T(1024)} %param.14, f32[128]{0:T(128)S(1)} %add_rsqrt_fusion.1, f32[128]{0:T(128)S(1)} %broadcast_multiply_fusion), kind=kOutput, calls=%fused_computation.67 | convolution fusion | flops 425738240 | bytes 4271104 | tf_op jit(solution)/shard_map/dot_general | solution.py:122
  13.4 0.0 all-reduce.2.cloned.1.call-update
  13.5 0.0 copy-start.6
  13.5 0.0 all-gather.5.cloned.1.call-start
  13.5 69.3 %all-reduce.2.cloned.1.call-done = f32[128,1280]{1,0:T(8,128)} async-done(((f32[128,1280]{1,0:T(8,128)}), f32[128,1280]{1,0:T(8,128)}) %all-reduce.2.cloned.1.call-update) | async-done | bytes 655376 | tf_op jit(solution)/shard_map/psum | solution.py:123
  82.8 0.0 copy-done
  82.8 0.0 copy-done.2
  82.9 2.3 convolution_convert_fusion
  85.2 0.0 all-gather.5.cloned.1.call-update
  85.2 0.0 reduce-scatter.2.cloned.1.call-start
  85.2 0.0 copy-done.4
  85.3 0.1 broadcast_bitcast_fusion.2
  85.3 0.1 broadcast_bitcast_fusion
  85.4 34.6 %all-gather.5.cloned.1.call-done = bf16[512,1024]{1,0:T(8,128)(2,1)} async-done(((bf16[128,1024]{1,0:T(8,128)(2,1)}), bf16[512,1024]{1,0:T(8,128)(2,1)}) %all-gather.5.cloned.1.call-update) | async-done | bytes 1048592 | tf_op jit(solution)/shard_map/all_gather | solution.py:131
  120.0 1.3 fusion.127
  121.3 0.0 copy-done.3
  121.3 1.6 fusion.19
  122.8 14.3 %psum.15 = f32[256]{0:T(256)S(1)} all-reduce(f32[256]{0:T(256)S(1)} %get-tuple-element.38), channel_id=1, replica_groups=mesh['sect'=4,'ctx'=8,'tp'=8] {'tp'}, use_global_device_ids=true, to_apply=%region_4.5 | all-reduce | flops 256 | bytes 2048 | tf_op jit(solution)/shard_map/psum | solution.py:140
  137.2 0.0 copy-done.6
  137.2 5.1 %convolution_bitcast_fusion = f32[2048,256]{0,1:T(8,128)} fusion(bf16[2048,1024]{1,0:T(8,128)(2,1)} %param.22, bf16[256,1024]{1,0:T(8,128)(2,1)} %get-tuple-element.39, f32[1024]{0:T(1024)S(1)} %copy-done.6, f32[256]{0:T(256)S(1)} %add_rsqrt_fusion), kind=kOutput, calls=%fused_computation.19 | convolution fusion | flops 1074790400 | bytes 6820864 | tf_op jit(solution)/shard_map/dot_general | solution.py:145
  142.3 0.0 reduce-scatter.2.cloned.1.call-update
  142.3 0.0 all-gather.7.cloned.1.call-start
  142.4 31.3 %reduce-scatter.2.cloned.1.call-done = f32[256,256]{0,1:T(8,128)} async-done(((f32[2048,256]{0,1:T(8,128)}), f32[256,256]{0,1:T(8,128)}) %reduce-scatter.2.cloned.1.call-update) | async-done | bytes 262160 | tf_op jit(solution)/shard_map/reduce_scatter | solution.py:144
  173.7 1.1 copy.20
  174.8 0.3 fusion.93
  175.1 0.6 pad_maximum_fusion
  175.7 0.0 all-gather.7.cloned.1.call-update
  175.8 0.2 all-gather.9.cloned.1.call-start
  176.0 0.6 slice.47
  176.6 0.0 all-gather.9.cloned.1.call-update
  176.6 73.0 %all-gather.7.cloned.1.call-done = bf16[1,128,8192]{2,1,0:T(8,128)(2,1)} async-done(((bf16[1,128,256]{2,1,0:T(8,128)(2,1)}), bf16[1,128,8192]{2,1,0:T(8,128)(2,1)}) %all-gather.7.cloned.1.call-update) | async-done | bytes 2097168 | tf_op jit(solution)/shard_map/all_gather | solution.py:170
  249.6 76.4 %all-gather.9.cloned.1.call-done = bf16[1,1,128,8192]{3,2,1,0:T(8,128)(2,1)} async-done(((bf16[1,1,128,256]{3,2,1,0:T(8,128)(2,1)}), bf16[1,1,128,8192]{3,2,1,0:T(8,128)(2,1)}) %all-gather.9.cloned.1.call-update) | async-done | bytes 2097168 | tf_op jit(solution)/shard_map/all_gather | solution.py:171
  326.1 0.0 copy-done.5
  326.1 49.8 %conditional.1 = (f32[1,4,256]{2,1,0:T(4,128)S(1)}, f32[1,4,256,128]{3,2,1,0:T(8,128)S(1)}) conditional(s32[]{:T(128)} %convert_element_type.65, () %tuple.13, (s32[]{:T(128)}, s32[256]{0:T(256)S(1)}, s32[8192]{0:T(1024)S(1)}, bf16[1,128,8192]{2,1,0:T(8,128)(2,1)}, bf16[256,512]{1,0:T(8,128)(2,1)S(1)}, ...), branch_computations={%region_6.7_spmd, %region_7.10_spmd} | conditional | flops 4389338112 | bytes 122481712 | solution.py:86
  326.1 3.7 broadcast_compare_fusion
  329.8 0.0 copy-start.1
  329.8 15.6 %fusion.2 = (f32[4,256]{1,0:T(4,128)S(1)}, f32[8192,256,4]{1,0,2:T(8,128)}) fusion(pred[256,8192]{0,1:T(8,128)(4,1)S(1)} %broadcast_compare_fusion, bf16[1,128,8192]{2,1,0:T(8,128)(2,1)} %get-tuple-element.35, bf16[256,512]{1,0:T(8,128)(2,1)S(1)} %get-tuple-element.31), kind=kOutput, calls=%fused_computation.4 | convolution fusion | flops 2172648448 | bytes 38014976 | tf_op jit(solution)/shard_map/cond/branch_1_fun/rkgd,kdn->kgrn/dot_general | solution.py:47
  345.5 0.0 copy-done.1
  345.5 15.8 %fusion.10 = f32[1,4,256,128]{3,2,1,0:T(8,128)S(1)} fusion(bf16[1,128,8192]{2,1,0:T(8,128)(2,1)} %get-tuple-element.25, f32[8192,256,4]{1,0,2:T(8,128)} %get-tuple-element.41, f32[4,256]{1,0:T(4,128)S(1)} %broadcast_maximum_fusion, pred[256,8192]{0,1:T(8,128)(4,1)} %copy-done.1), kind=kOutput, calls=%fused_computation.12 | convolution fusion | flops 2181038080 | bytes 38277120 | tf_op jit(solution)/shard_map/cond/branch_1_fun/kgrn,kdn->kgrd/dot_general | solution.py:55
  361.2 14.6 %fusion.1 = f32[4,256]{1,0:T(4,128)S(1)} fusion(f32[8192,256,4]{1,0,2:T(8,128)} %get-tuple-element.41, f32[4,256]{1,0:T(4,128)S(1)} %broadcast_maximum_fusion, pred[256,8192]{0,1:T(8,128)(4,1)} %copy-done.1), kind=kLoop, calls=%fused_computation.3 | loop fusion | flops 33553408 | bytes 35659776 | tf_op jit(solution)/shard_map/cond/branch_1_fun/reduce_sum | solution.py:54
  375.9 0.2 fusion.57
  376.1 0.2 copy.22
  376.3 0.7 copy.33
  (14 shorter events, 0.1 us)
Async XLA Ops:
  6.5 76.3 %copy-start = (bf16[1280,1024]{1,0:T(8,128)(2,1)S(1)}, bf16[1280,1024]{1,0:T(8,128)(2,1)}, u32[]{:S(2)}) copy-start(bf16[1280,1024]{1,0:T(8,128)(2,1)} %param.18) | copy-start | bytes 7864324
  6.5 76.3 %all-reduce.2.cloned.1.call-start = ((), (), s32[]{:S(2)}) async-start(), calls=%async_computation.1 | async-start | bytes 1310720 | tf_op jit(solution)/shard_map/psum | solution.py:123
  9.0 73.8 %copy-start.2 = (bf16[128,1280]{1,0:T(8,128)(2,1)S(1)}, bf16[128,1280]{1,0:T(8,128)(2,1)}, u32[]{:S(2)}) copy-start(bf16[128,1280]{1,0:T(8,128)(2,1)} %param.13) | copy-start | bytes 983044
  13.4 71.8 %copy-start.4 = (s32[2]{0:T(128)S(1)}, s32[2]{0:T(128)}, u32[]{:S(2)}) copy-start(s32[2]{0:T(128)} %param.20) | copy-start | bytes 28
  13.4 107.8 %copy-start.3 = (bf16[256,1024]{1,0:T(8,128)(2,1)S(1)}, bf16[256,1024]{1,0:T(8,128)(2,1)}, u32[]{:S(2)}) copy-start(bf16[256,1024]{1,0:T(8,128)(2,1)} %param.19) | copy-start | bytes 1572868
  13.5 123.7 %copy-start.6 = (f32[1024]{0:T(1024)S(1)}, f32[1024]{0:T(1024)}, u32[]{:S(2)}) copy-start(f32[1024]{0:T(1024)} %param.21) | copy-start | bytes 12292
  13.5 106.5 %all-gather.5.cloned.1.call-start = ((), (), s32[]{:S(2)}) async-start(), calls=%async_computation.2 | async-start | bytes 1310720 | tf_op jit(solution)/shard_map/all_gather | solution.py:131
  85.2 88.5 %reduce-scatter.2.cloned.1.call-start = ((), (), s32[]{:S(2)}) async-start(), calls=%async_computation.3 | async-start | bytes 2359296 | tf_op jit(solution)/shard_map/reduce_scatter | solution.py:144
  137.2 188.9 %copy-start.5 = (bf16[256,512]{1,0:T(8,128)(2,1)S(1)}, bf16[256,512]{1,0:T(8,128)(2,1)}, u32[]{:S(2)}) copy-start(bf16[256,512]{1,0:T(8,128)(2,1)} %param.23) | copy-start | bytes 786436
  142.3 107.3 %all-gather.7.cloned.1.call-start = ((), (), s32[]{:S(2)}) async-start(), calls=%async_computation.4 | async-start | bytes 2162688 | tf_op jit(solution)/shard_map/all_gather | solution.py:170
  175.8 150.3 %all-gather.9.cloned.1.call-start = ((), (), s32[]{:S(2)}) async-start(), calls=%async_computation.5 | async-start | bytes 2162688 | tf_op jit(solution)/shard_map/all_gather | solution.py:171
  329.8 15.6 %copy-start.1 = (pred[256,8192]{0,1:T(8,128)(4,1)}, pred[256,8192]{0,1:T(8,128)(4,1)S(1)}, u32[]{:S(2)}) copy-start(pred[256,8192]{0,1:T(8,128)(4,1)S(1)} %broadcast_compare_fusion) | copy-start | bytes 6291460 | tf_op jit(solution)/shard_map/cond
Sparse Core Ops, SparseCore 0:
  13.6 69.2 all-reduce.1
  85.3 34.6 all-gather.4
  142.4 31.1 reduce-scatter.1
  176.0 73.6 all-gather.6
  252.0 74.0 all-gather.8
where the time goes:
time: 384 us
  waiting for transfers between devices  285 us (74%)
  matrix products  43.2 us (11%)
  other arithmetic  23.6 us (6%)
  blocking collectives  14.3 us (4%)
  between operations  13.3 us (3%)
  local copies, waits for them, and re-layouts  4.12 us (1%)
    all_gather x1, waiting for transfers between devices, body(): lax.all_gather(value_rows, ('sect', 'ctx'), axis=2, tiled=True)  76.4 us
    all_gather x1, waiting for transfers between devices, body(): lax.all_gather(rotated, ('sect', 'ctx'), axis=2, tiled=True)  73 us
    psum x1, waiting for transfers between devices, body(): summed_out = lax.psum(partial_out, 'tp')  69.3 us
    all_gather x1, waiting for transfers between devices, body(): fragment = lax.all_gather(image_emb, 'sect', axis=0, tiled=True)  34.6 us
    reduce_scatter x1, waiting for transfers between devices, body(): lax.psum_scatter(lax.dot_general(kv_weight, normed_hidden, (((1,), (1,)),...  31.3 us
    dot_general x1, matrix products, attend_update(): jnp.einsum('kgrn,kdn->kgrd', weights.astype(jnp.bfloat16), values_blk, pr...  15.8 us
    dot_general x1, matrix products, attend_update(): jnp.einsum('rkgd,kdn->kgrn', queries_blk, keys_blk, preferred_element_typ...  15.6 us
    reduce_sum x1, other arithmetic, attend_update(): running_sum = jnp.sum(weights, axis=-1)  14.6 us
  transfers between devices with their start and end apart: 5, of which 5 were waited for; matrix products, arithmetic and copies ran while one was open for 0% of the time, Pallas kernels for 0%

commit v1 on v0

--- a/solution.py
+++ b/solution.py
@@ -1,3 +1,4 @@
+import functools
 from functools import partial
 import math
 import jax
@@ -10,6 +11,15 @@
 Q_HEADS = 32
 KV_HEADS = 8
 PATCHES = 128
+
+
+def handle_modes(base_x, device_axis):
+    return jnp.concatenate(
+        lax.all_to_all(jnp.stack(lax.psum(1, device_axis) * [base_x], 0), device_axis, 0, 0), 2
+    )
+
+
+layers_all_use = functools.partial(handle_modes, device_axis=("sect", "ctx"))
 
 
 def layer_norm(values, norm_scale, norm_shift):
@@ -166,10 +176,7 @@
     folder = partial(fold_step, groups=groups)
     finals = folder(
         initial,
-        (
-            lax.all_gather(rotated, ("sect", "ctx"), axis=2, tiled=True),
-            lax.all_gather(value_rows, ("sect", "ctx"), axis=2, tiled=True),
-        ),
+        (layers_all_use(rotated), lax.all_gather(value_rows, ("sect", "ctx"), axis=2, tiled=True)),
         jnp.int32(0),
     )
     results = [finish_state(state_now) for state_now in finals]

time: 384 us -> 325 us (0.85)
  waiting for transfers between devices: 285 us -> 214 us
  starting transfers between devices: 0.35 us -> 10.3 us
    all_gather x1 -> x0, waiting for transfers between devices: 73 us -> none  [body(): lax.all_gather(rotated, ('sect', 'ctx'), axis=2, tiled=True)]
    all_to_all x0 -> x1, starting transfers between devices: none -> 10.1 us  [handle_modes(): lax.all_to_all(jnp.stack(lax.psum(1, device_axis) * [base_x], 0), device_...]
  transfers between devices with their start and end apart: 5 -> 5, of which waited for: 5 -> 4; matrix products, arithmetic and copies ran while one was open for 0% -> 1% of each run, Pallas kernels for 0% -> 0%
where the time goes in v1:
time: 325 us
  waiting for transfers between devices  214 us (66%)
  matrix products  43.1 us (13%)
  other arithmetic  23.3 us (7%)
  blocking collectives  14.3 us (4%)
  between operations  13.3 us (4%)
  starting transfers between devices  10.3 us (3%)
  local copies, waits for them, and re-layouts  6.3 us (2%)
    all_gather x1, waiting for transfers between devices, body(): lax.all_gather(value_rows, ('sect', 'ctx'), axis=2, tiled=True)  79.1 us
    psum x1, waiting for transfers between devices, body(): summed_out = lax.psum(partial_out, 'tp')  69.3 us
    all_gather x1, waiting for transfers between devices, body(): fragment = lax.all_gather(image_emb, 'sect', axis=0, tiled=True)  34.6 us
    reduce_scatter x1, waiting for transfers between devices, body(): lax.psum_scatter(lax.dot_general(kv_weight, normed_hidden, (((1,), (1,)),...  31.3 us
    dot_general x1, matrix products, attend_update(): jnp.einsum('kgrn,kdn->kgrd', weights.astype(jnp.bfloat16), values_blk, pr...  15.8 us
    dot_general x1, matrix products, attend_update(): jnp.einsum('rkgd,kdn->kgrn', queries_blk, keys_blk, preferred_element_typ...  15.6 us
    reduce_sum x1, other arithmetic, attend_update(): running_sum = jnp.sum(weights, axis=-1)  14.6 us
    psum x1, blocking collectives, body(): square_sums = lax.psum(jnp.sum(jnp.square(widened), axis=1), 'tp')  14.3 us
  transfers between devices with their start and end apart: 5, of which 4 were waited for; matrix products, arithmetic and copies ran while one was open for 1% of the time, Pallas kernels for 0%

profile of v1, /device:TPU:8, one launch (start us, length us, event | category | flops | bytes accessed | tf_op | source)
XLA Modules:
  0.0 325.0 jit_solution(3339055922543097875)
XLA Ops:
  6.5 0.0 copy-start
  6.5 0.0 all-reduce.2.cloned.1.call-start
  6.5 1.2 convert_reduce_fusion
  7.8 1.2 fusion.23
  9.0 4.4 %fusion.54 = f32[128,1280]{1,0:T(8,128)} fusion(bf16[640,1280]{1,0:T(8,128)(2,1)} %param.17, bf16[1280,640]{1,0:T(8,128)(2,1)} %param.16, bf16[128,1280]{1,0:T(8,128)(2,1)} %param.13, f32[1280]{0:T(1024)} %param.15, f32[1280]{0:T(1024)} %param.14, f32[128]{0:T(128)S(1)} %add_rsqrt_fusion.1, f32[128]{0:T(128)S(1)} %broadcast_multiply_fusion), kind=kOutput, calls=%fused_computation.66 | convolution fusion | flops 425738240 | bytes 4271104 | tf_op jit(solution)/shard_map/dot_general | solution.py:132
  13.4 0.0 all-reduce.2.cloned.1.call-update
  13.5 0.0 copy-start.6
  13.5 0.0 all-gather.4.cloned.1.call-start
  13.5 69.3 %all-reduce.2.cloned.1.call-done = f32[128,1280]{1,0:T(8,128)} async-done(((f32[128,1280]{1,0:T(8,128)}), f32[128,1280]{1,0:T(8,128)}) %all-reduce.2.cloned.1.call-update) | async-done | bytes 655376 | tf_op jit(solution)/shard_map/psum | solution.py:133
  82.9 0.0 copy-done
  82.9 0.0 copy-done.2
  82.9 2.3 convolution_convert_fusion
  85.2 0.0 all-gather.4.cloned.1.call-update
  85.2 0.0 reduce-scatter.2.cloned.1.call-start
  85.2 0.0 copy-done.4
  85.3 0.1 broadcast_bitcast_fusion.2
  85.3 0.1 broadcast_bitcast_fusion
  85.4 34.6 %all-gather.4.cloned.1.call-done = bf16[512,1024]{1,0:T(8,128)(2,1)} async-done(((bf16[128,1024]{1,0:T(8,128)(2,1)}), bf16[512,1024]{1,0:T(8,128)(2,1)}) %all-gather.4.cloned.1.call-update) | async-done | bytes 1048592 | tf_op jit(solution)/shard_map/all_gather | solution.py:141
  120.0 1.3 fusion.128
  121.3 0.0 copy-done.3
  121.3 1.6 fusion.18
  122.9 14.3 %psum.15 = f32[256]{0:T(256)S(1)} all-reduce(f32[256]{0:T(256)S(1)} %get-tuple-element.39), channel_id=1, replica_groups=mesh['sect'=4,'ctx'=8,'tp'=8] {'tp'}, use_global_device_ids=true, to_apply=%region_4.5 | all-reduce | flops 256 | bytes 2048 | tf_op jit(solution)/shard_map/psum | solution.py:150
  137.2 0.0 copy-done.6
  137.2 5.1 %convolution_bitcast_fusion = f32[2048,256]{0,1:T(8,128)} fusion(bf16[2048,1024]{1,0:T(8,128)(2,1)} %param.22, bf16[256,1024]{1,0:T(8,128)(2,1)} %get-tuple-element.40, f32[1024]{0:T(1024)S(1)} %copy-done.6, f32[256]{0:T(256)S(1)} %add_rsqrt_fusion), kind=kOutput, calls=%fused_computation.18 | convolution fusion | flops 1074790400 | bytes 6820864 | tf_op jit(solution)/shard_map/dot_general | solution.py:155
  142.3 0.0 reduce-scatter.2.cloned.1.call-update
  142.3 0.0 copy-start.5
  142.3 0.0 all-gather.6.cloned.1.call-start
  142.4 31.3 %reduce-scatter.2.cloned.1.call-done = f32[256,256]{0,1:T(8,128)} async-done(((f32[2048,256]{0,1:T(8,128)}), f32[256,256]{0,1:T(8,128)}) %reduce-scatter.2.cloned.1.call-update) | async-done | bytes 262160 | tf_op jit(solution)/shard_map/reduce_scatter | solution.py:154
  173.6 1.1 reshape.221
  174.7 0.1 slice.40
  174.9 0.1 slice.37
  175.0 0.7 copy.23
  175.7 0.0 all-gather.6.cloned.1.call-update
  175.7 0.6 fusion.96
  176.3 0.1 pad_maximum_fusion
  176.4 1.8 stack.2
  178.3 10.1 %all-to-all-start = ((bf16[32,1,128,256]{2,3,1,0:T(8,128)(2,1)}), bf16[32,1,128,256]{2,3,1,0:T(8,128)(2,1)}, u32[]{:S(2)}, u32[]{:S(2)}) async-start(bf16[32,1,128,256]{2,3,1,0:T(8,128)(2,1)} %stack.2), calls=%async_computation.1 | async-start | bytes 4194304 | tf_op jit(solution)/shard_map/all_to_all | solution.py:18
  188.4 79.1 %all-gather.6.cloned.1.call-done = bf16[1,1,128,8192]{3,2,1,0:T(8,128)(2,1)} async-done(((bf16[1,1,128,256]{3,2,1,0:T(8,128)(2,1)}), bf16[1,1,128,8192]{3,2,1,0:T(8,128)(2,1)}) %all-gather.6.cloned.1.call-update) | async-done | bytes 2097168 | tf_op jit(solution)/shard_map/all_gather | solution.py:179
  267.5 0.0 all-to-all-done
  267.5 49.8 %conditional.1 = (f32[1,4,256]{2,1,0:T(4,128)S(1)}, f32[1,4,256,128]{3,2,1,0:T(8,128)S(1)}) conditional(s32[]{:T(128)} %convert_element_type.64, () %tuple.13, (s32[]{:T(128)}, s32[256]{0:T(256)S(1)}, s32[8192]{0:T(1024)S(1)}, bf16[1,128,32,256]{1,3,0,2:T(8,128)(2,1)}, bf16[256,512]{1,0:T(8,128)(2,1)S(1)}, ...), branch_computations={%region_6.7_spmd, %region_7.10_spmd} | conditional | flops 4389338112 | bytes 122481712 | solution.py:96
  267.5 3.7 %broadcast_compare_fusion = pred[256,8192]{0,1:T(8,128)(4,1)S(1)} fusion(s32[256]{0:T(256)S(1)} %broadcast_add_fusion, s32[8192]{0:T(1024)S(1)} %get-tuple-element.23), kind=kLoop, calls=%fused_computation.8 | loop fusion | flops 2097152 | bytes 2130944 | tf_op jit(solution)/shard_map/cond/branch_1_fun/ge | solution.py:60
  271.3 15.6 %fusion.2 = (f32[4,256]{1,0:T(4,128)S(1)}, f32[8192,256,4]{1,0,2:T(8,128)}) fusion(pred[256,8192]{0,1:T(8,128)(4,1)S(1)} %broadcast_compare_fusion, bf16[128,8192,1]{0,1,2:T(8,128)(2,1)} %bitcast.2, bf16[256,512]{1,0:T(8,128)(2,1)S(1)} %get-tuple-element.32), kind=kOutput, calls=%fused_computation.4 | convolution fusion | flops 2172648448 | bytes 38014976 | tf_op jit(solution)/shard_map/cond/branch_1_fun/rkgd,kdn->kgrn/dot_general | solution.py:57
  286.8 0.0 copy-done.1
  286.9 15.8 %fusion.8 = f32[1,4,256,128]{3,2,1,0:T(8,128)S(1)} fusion(bf16[1,128,8192]{2,1,0:T(8,128)(2,1)} %get-tuple-element.26, f32[8192,256,4]{1,0,2:T(8,128)} %get-tuple-element.42, f32[4,256]{1,0:T(4,128)S(1)} %broadcast_maximum_fusion, pred[256,8192]{0,1:T(8,128)(4,1)} %copy-done.1), kind=kOutput, calls=%fused_computation.10 | convolution fusion | flops 2181038080 | bytes 38277120 | tf_op jit(solution)/shard_map/cond/branch_1_fun/kgrn,kdn->kgrd/dot_general | solution.py:65
  302.7 14.6 %fusion.1 = f32[4,256]{1,0:T(4,128)S(1)} fusion(f32[8192,256,4]{1,0,2:T(8,128)} %get-tuple-element.42, f32[4,256]{1,0:T(4,128)S(1)} %broadcast_maximum_fusion, pred[256,8192]{0,1:T(8,128)(4,1)} %copy-done.1), kind=kLoop, calls=%fused_computation.3 | loop fusion | flops 33553408 | bytes 35659776 | tf_op jit(solution)/shard_map/cond/branch_1_fun/reduce_sum | solution.py:64
  317.3 0.2 fusion.56
  317.5 0.2 copy.21
  317.7 0.7 copy.33
  (15 shorter events, 0.1 us)
Async XLA Ops:
  6.5 76.3 %copy-start = (bf16[1280,1024]{1,0:T(8,128)(2,1)S(1)}, bf16[1280,1024]{1,0:T(8,128)(2,1)}, u32[]{:S(2)}) copy-start(bf16[1280,1024]{1,0:T(8,128)(2,1)} %param.18) | copy-start | bytes 7864324
  6.5 76.3 %all-reduce.2.cloned.1.call-start = ((), (), s32[]{:S(2)}) async-start(), calls=%async_computation.2 | async-start | bytes 1310720 | tf_op jit(solution)/shard_map/psum | solution.py:133
  9.0 73.8 %copy-start.2 = (bf16[128,1280]{1,0:T(8,128)(2,1)S(1)}, bf16[128,1280]{1,0:T(8,128)(2,1)}, u32[]{:S(2)}) copy-start(bf16[128,1280]{1,0:T(8,128)(2,1)} %param.13) | copy-start | bytes 983044
  13.4 71.8 %copy-start.4 = (s32[2]{0:T(128)S(1)}, s32[2]{0:T(128)}, u32[]{:S(2)}) copy-start(s32[2]{0:T(128)} %param.20) | copy-start | bytes 28
  13.4 107.8 %copy-start.3 = (bf16[256,1024]{1,0:T(8,128)(2,1)S(1)}, bf16[256,1024]{1,0:T(8,128)(2,1)}, u32[]{:S(2)}) copy-start(bf16[256,1024]{1,0:T(8,128)(2,1)} %param.19) | copy-start | bytes 1572868
  13.5 123.7 %copy-start.6 = (f32[1024]{0:T(1024)S(1)}, f32[1024]{0:T(1024)}, u32[]{:S(2)}) copy-start(f32[1024]{0:T(1024)} %param.21) | copy-start | bytes 12292
  13.5 106.5 %all-gather.4.cloned.1.call-start = ((), (), s32[]{:S(2)}) async-start(), calls=%async_computation.3 | async-start | bytes 1310720 | tf_op jit(solution)/shard_map/all_gather | solution.py:141
  85.2 88.5 %reduce-scatter.2.cloned.1.call-start = ((), (), s32[]{:S(2)}) async-start(), calls=%async_computation.4 | async-start | bytes 2359296 | tf_op jit(solution)/shard_map/reduce_scatter | solution.py:154
  142.3 125.2 %copy-start.5 = (bf16[256,512]{1,0:T(8,128)(2,1)S(1)}, bf16[256,512]{1,0:T(8,128)(2,1)}, u32[]{:S(2)}) copy-start(bf16[256,512]{1,0:T(8,128)(2,1)} %param.23) | copy-start | bytes 786436
  142.3 125.2 %all-gather.6.cloned.1.call-start = ((), (), s32[]{:S(2)}) async-start(), calls=%async_computation.5 | async-start | bytes 2162688 | tf_op jit(solution)/shard_map/all_gather | solution.py:179
  178.3 89.2 %all-to-all-start = ((bf16[32,1,128,256]{2,3,1,0:T(8,128)(2,1)}), bf16[32,1,128,256]{2,3,1,0:T(8,128)(2,1)}, u32[]{:S(2)}, u32[]{:S(2)}) async-start(bf16[32,1,128,256]{2,3,1,0:T(8,128)(2,1)} %stack.2), calls=%async_computation.1 | async-start | bytes 4194304 | tf_op jit(solution)/shard_map/all_to_all | solution.py:18
  271.3 15.6 %copy-start.1 = (pred[256,8192]{0,1:T(8,128)(4,1)}, pred[256,8192]{0,1:T(8,128)(4,1)S(1)}, u32[]{:S(2)}) copy-start(pred[256,8192]{0,1:T(8,128)(4,1)S(1)} %broadcast_compare_fusion) | copy-start | bytes 6291460 | tf_op jit(solution)/shard_map/cond
Sparse Core Ops, SparseCore 0:
  13.6 69.2 all-reduce.1
  85.3 34.6 all-gather.3
  142.4 31.1 reduce-scatter.1
  176.0 91.4 all-gather.5
